TPU v7x, 512 devices: a whole 4x4x16 slice. The times are simulated.
512 devices in a mesh: day: 64 (over z, y), pair: 8 (over x, core).
Axes of the slice: x: 4, y: 4, z: 16, core: 2. Of those that a mesh axis runs over, the one named last changes fastest.
Arguments:
- spectra: bfloat16 [128, 128, 4096], P('day', 'pair'), may hold values from -40 to 40
- pair_stations: int32 [512, 2], P('pair'), may hold values from 0 to 127
- availability: int32 [128, 128], P('day'), may hold values from 0 to 1
Outputs:
- stacks: bfloat16 [128, 512, 1001], P('day', 'pair')
- reference: float32 [512, 1001], P('pair')
All inputs are finite; a program needn't handle non-finite values.
Results may differ from a plain program's by a relative error of at most 0.008.
Values may be sent and summed in bfloat16 or wider, within the bound.
A program may use at most 64 MiB of HBM per device.

v0:
```python
import jax
import jax.numpy as jnp
import numpy as np
from jax import lax
from jax.sharding import PartitionSpec as P

LAGS = 1001
WIDE = 1024
WINDOW = 30


def lag_table(bin_count):
    bin_ids = np.arange(bin_count)[:, None]
    lag_ids = np.arange(LAGS)[None, :] - (LAGS - 1) // 2
    angle = np.mod(bin_ids * lag_ids, 2 * bin_count) * (np.pi / bin_count)
    factor = 1.0 / np.sqrt(2.0 * bin_count)
    table = np.concatenate([np.cos(angle) * factor, -np.sin(angle) * factor], 0)
    return np.pad(table, ((0, 0), (0, WIDE - LAGS))).astype(np.float32).astype(jnp.bfloat16)


def per_device(spectra, pair_stations, availability):
    days_here = spectra.shape[0]
    groups = lax.axis_size("day")
    station_count = spectra.shape[1] * lax.axis_size("pair")
    bin_count = spectra.shape[2] // 2
    pairs_here = pair_stations.shape[0]
    inverse = jnp.asarray(lag_table(bin_count))
    station_ids = jnp.arange(station_count, dtype=jnp.int32)
    ends = jnp.concatenate([pair_stations[:, 0], pair_stations[:, 1]], 0)
    pick = (ends[:, None] == station_ids[None, :]).astype(jnp.bfloat16)
    avail = jnp.dot(availability.astype(jnp.bfloat16), pick.T, preferred_element_type=jnp.float32)
    present = avail[:, :pairs_here] * avail[:, pairs_here:]
    gathered = lax.all_gather(spectra, "pair", axis=1, tiled=True)
    rows = []
    for day in range(days_here):
        spec = jnp.dot(pick, gathered[day], preferred_element_type=jnp.float32)
        one, two = (spec[:pairs_here], spec[pairs_here:])
        ar, ai, br, bi = (
            one[:, :bin_count],
            one[:, bin_count:],
            two[:, :bin_count],
            two[:, bin_count:],
        )
        rows.append(jnp.concatenate([ar * br + ai * bi, ar * bi - ai * br], 1).astype(jnp.bfloat16))
    cross = jnp.concatenate(rows, 0)
    corr = jnp.dot(cross, inverse, preferred_element_type=jnp.float32)
    column = lax.broadcasted_iota(jnp.int32, (1, WIDE), 1)
    shown = present.reshape(-1, 1)
    daily = jnp.where(column == LAGS, shown, corr * shown).astype(jnp.bfloat16)
    daily = daily.reshape(days_here, pairs_here, WIDE)
    turned = lax.all_to_all(daily, "day", split_axis=1, concat_axis=0, tiled=True)
    days = groups * days_here
    mine = turned.reshape(days, WIDE)
    day_ids = np.arange(days)
    gap = day_ids[:, None] - day_ids[None, :]
    band = jnp.asarray(((gap >= 0) & (gap < WINDOW)).astype(np.float32), dtype=jnp.bfloat16)
    moving = jnp.dot(band, mine, preferred_element_type=jnp.float32)
    counts = moving[:, LAGS : LAGS + 1]
    ref = jnp.sum(mine.astype(jnp.float32), axis=0) / days
    ref = jnp.where(column[0] < LAGS, ref, 0.0)
    scale = jnp.sqrt(jnp.sum(ref * ref) / LAGS + 1e-06)
    stacks = (moving / jnp.maximum(counts, 1.0) / scale).astype(jnp.bfloat16)
    back = lax.all_to_all(
        stacks.reshape(days, 1, WIDE), "day", split_axis=0, concat_axis=1, tiled=True
    )
    ref_all = lax.all_gather(ref[None], "day", axis=0, tiled=True)
    return (back[:, :, :LAGS], ref_all[:, :LAGS])


def solution(mesh):
    return jax.shard_map(
        per_device,
        mesh=mesh,
        in_specs=(P("day", "pair", None), P("pair", None), P("day", None)),
        out_specs=(P("day", "pair", None), P("pair", None)),
        check_vma=False,
    )
```

profile of v0, /device:TPU:8, one launch (start us, length us, event | category | flops | bytes accessed | tf_op | source)
XLA Modules:
  0.0 198.5 jit_solution(13838983268094882941)
XLA Ops:
  7.2 0.0 all-gather.3.cloned.1.call-start
  7.2 0.7 all-gather.3.cloned.1.call-update
  7.9 0.8 slice_bitcast_fusion.5
  8.7 0.1 pad_add_fusion
  8.7 0.9 convolution_bitcast_fusion
  9.6 0.1 slice_multiply_fusion
  9.7 0.1 broadcast_in_dim.28
  9.8 37.6 %all-gather.3.cloned.1.call-done = bf16[2,128,4096]{2,1,0:T(8,128)(2,1)} async-done(((bf16[2,16,4096]{2,1,0:T(8,128)(2,1)}), bf16[2,128,4096]{2,1,0:T(8,128)(2,1)}) %all-gather.3.cloned.1.call-update) | async-done | bytes 2097168 | tf_op jit(solution)/shard_map/all_gather | solution.py:33
  47.4 1.8 fusion.3
  49.2 0.1 copy-done
  49.3 0.5 fusion.2
  49.8 0.4 add_convert_fusion
  50.2 2.5 %copy-done.2 = bf16[4096,1024]{1,0:T(8,128)(2,1)S(1)} copy-done((bf16[4096,1024]{1,0:T(8,128)(2,1)S(1)}, bf16[4096,1024]{1,0:T(8,128)(2,1)}, u32[]{:S(2)}) %copy-start.2) | copy-done | bytes 8388632
  52.7 1.3 fusion.1
  54.0 0.3 copy.12
  54.3 37.4 %all_to_all.33 = bf16[2,64,1024]{2,0,1:T(2,128)(2,1)S(1)} all-to-all(bf16[2,64,1024]{2,0,1:T(2,128)(2,1)S(1)} %copy.12), channel_id=1, replica_groups=mesh['day'=64,'pair'=8] {'day'}, dimensions={1} | all-to-all | bytes 524288 | tf_op jit(solution)/shard_map/all_to_all | solution.py:51
  91.7 0.2 convert_reduce_fusion
  91.9 0.6 broadcast_multiply_fusion
  93.3 0.2 fusion.18
  93.5 0.2 fusion.11
  93.7 0.1 fusion.9
  93.8 0.5 broadcast.36
  94.3 0.8 reduce.6
  95.1 0.8 reshape.58
  95.9 5.9 %all-to-all-start.1 = ((bf16[64,2,1024]{2,1,0:T(2,128)(2,1)}), bf16[64,2,1024]{2,1,0:T(2,128)(2,1)S(1)}, u32[]{:S(2)}, u32[]{:S(2)}) async-start(bf16[64,2,1024]{2,1,0:T(2,128)(2,1)} %reshape.58), calls=%async_computation.1 | async-start | bytes 524288 | tf_op jit(solution)/shard_map/all_to_all | solution.py:63
  101.9 86.4 %all-gather = f32[64,1,1024]{2,1,0:T(1,128)S(1)} all-gather(f32[1,1,1024]{2,1,0:T(1,128)S(1)} %fusion.15), channel_id=1, replica_groups=mesh['day'=64,'pair'=8] {'day'}, dimensions={0}, use_global_device_ids=true | all-gather | bytes 266240 | tf_op jit(solution)/shard_map/all_gather | solution.py:66
  188.3 0.8 copy.19
  189.1 0.0 all-to-all-done.1
  189.1 0.2 reshape.59
  189.3 1.5 reduce.4
  190.8 0.1 all_to_all.28
  190.9 0.8 copy.15
  (7 shorter events, 0.1 us)
Async XLA Ops:
  7.2 40.2 %all-gather.3.cloned.1.call-start = ((), (), s32[]{:S(2)}) async-start(), calls=%async_computation.2 | async-start | bytes 2359296 | tf_op jit(solution)/shard_map/all_gather | solution.py:33
  47.4 1.9 copy-start
  49.3 3.4 %copy-start.2 = (bf16[4096,1024]{1,0:T(8,128)(2,1)S(1)}, bf16[4096,1024]{1,0:T(8,128)(2,1)}, u32[]{:S(2)}) copy-start(bf16[4096,1024]{1,0:T(8,128)(2,1)} %constant.19.clone) | copy-start | bytes 25165828
  52.7 40.6 %copy-start.1 = (bf16[128,128]{1,0:T(8,128)(2,1)S(1)}, bf16[128,128]{1,0:T(8,128)(2,1)}, u32[]{:S(2)}) copy-start(bf16[128,128]{1,0:T(8,128)(2,1)} %constant.25) | copy-start | bytes 98308
  95.9 93.1 %all-to-all-start.1 = ((bf16[64,2,1024]{2,1,0:T(2,128)(2,1)}), bf16[64,2,1024]{2,1,0:T(2,128)(2,1)S(1)}, u32[]{:S(2)}, u32[]{:S(2)}) async-start(bf16[64,2,1024]{2,1,0:T(2,128)(2,1)} %reshape.58), calls=%async_computation.1 | async-start | bytes 524288 | tf_op jit(solution)/shard_map/all_to_all | solution.py:63
Sparse Core Ops, SparseCore 0:
  10.1 37.1 all-gather.2
where the time goes:
time: 199 us
  blocking collectives  124 us (62%)
  waiting for transfers between devices  38.3 us (19%)
  between operations  14.8 us (7%)
  local copies, waits for them, and re-layouts  6.83 us (3%)
  starting transfers between devices  5.97 us (3%)
  matrix products  4.73 us (2%)
  other arithmetic  4.04 us (2%)
    all_gather x1, blocking collectives, per_device(): ref_all = lax.all_gather(ref[None], 'day', axis=0, tiled=True)  86.4 us
    all_gather x1, waiting for transfers between devices, per_device(): gathered = lax.all_gather(spectra, 'pair', axis=1, tiled=True)  37.6 us
    all_to_all x1, blocking collectives, per_device(): lax.all_to_all(daily, 'day', split_axis=1, concat_axis=0, tiled=True)  37.4 us
    all_to_all x1, starting transfers between devices, per_device(): lax.all_to_all(stacks.reshape(days, 1, WIDE), 'day', split_axis=0, concat...  5.93 us
    unnamed x10, local copies, waits for them, and re-layouts  5.05 us
  transfers between devices with their start and end apart: 2, of which 1 were waited for; matrix products, arithmetic and copies ran while one was open for 1% of the time, Pallas kernels for 0%

commit v1 on v0

--- a/solution.py
+++ b/solution.py
@@ -7,6 +7,19 @@
 LAGS = 1001
 WIDE = 1024
 WINDOW = 30
+
+
+def collect(x, axis, dim):
+    ways = lax.axis_size(axis)
+    up = [(d, (d + 1) % ways) for d in range(ways)]
+    down = [(d, (d - 1) % ways) for d in range(ways)]
+    earlier, later = ([x], [x])
+    for _ in range(ways // 2):
+        earlier.append(lax.ppermute(earlier[-1], axis, up))
+    for _ in range((ways - 1) // 2):
+        later.append(lax.ppermute(later[-1], axis, down))
+    line = jnp.concatenate([*earlier[::-1], *later[1:]], axis=dim)
+    return jnp.roll(line, (lax.axis_index(axis) - ways // 2) * x.shape[dim], axis=dim)
 
 
 def lag_table(bin_count):
@@ -30,7 +43,7 @@
     pick = (ends[:, None] == station_ids[None, :]).astype(jnp.bfloat16)
     avail = jnp.dot(availability.astype(jnp.bfloat16), pick.T, preferred_element_type=jnp.float32)
     present = avail[:, :pairs_here] * avail[:, pairs_here:]
-    gathered = lax.all_gather(spectra, "pair", axis=1, tiled=True)
+    gathered = collect(spectra, "pair", 1)
     rows = []
     for day in range(days_here):
         spec = jnp.dot(pick, gathered[day], preferred_element_type=jnp.float32)

time: 199 us -> 173 us (0.87)
  the two profiles are of different devices: /device:TPU:8 before, /device:TPU:4 now
where the time goes in v1:
time: 173 us
  blocking collectives  129 us (75%)
  waiting for transfers between devices  16.1 us (9%)
  starting transfers between devices  11.2 us (6%)
  local copies, waits for them, and re-layouts  7.58 us (4%)
  other arithmetic  4.03 us (2%)
  matrix products  3.36 us (2%)
    all_gather x1, blocking collectives, per_device(): ref_all = lax.all_gather(ref[None], 'day', axis=0, tiled=True)  87.7 us
    all_to_all x1, blocking collectives, per_device(): lax.all_to_all(daily, 'day', split_axis=1, concat_axis=0, tiled=True)  41.4 us
    ppermute x4, waiting for transfers between devices, collect(): earlier.append(lax.ppermute(earlier[-1], axis, up))  15.4 us
    all_to_all x1, starting transfers between devices, per_device(): lax.all_to_all(stacks.reshape(days, 1, WIDE), 'day', split_axis=0, concat...  5.8 us
    unnamed x27, local copies, waits for them, and re-layouts  5.78 us
    ppermute x3, starting transfers between devices, collect(): later.append(lax.ppermute(later[-1], axis, down))  5.41 us
  transfers between devices with their start and end apart: 8, of which 5 were waited for; matrix products, arithmetic and copies ran while one was open for 2% of the time, Pallas kernels for 0%

profile of v1, /device:TPU:4, one launch (start us, length us, event | category | flops | bytes accessed | tf_op | source)
XLA Modules:
  0.0 173.0 jit_solution(4164248339607749585)
XLA Ops:
  0.7 6.0 %collective-permute-done = bf16[2,16,4096]{2,1,0:T(8,128)(2,1)S(1)} collective-permute-done((bf16[2,16,4096]{2,1,0:T(8,128)(2,1)}, bf16[2,16,4096]{2,1,0:T(8,128)(2,1)S(1)}, u32[]{:S(2)}, u32[]{:S(2)}) %collective-permute-start) | collective-permute-done | bytes 262176 | tf_op jit(solution)/shard_map/ppermute | solution.py:18
  6.7 1.7 %collective-permute-start.4 = (bf16[2,16,4096]{2,1,0:T(8,128)(2,1)}, bf16[2,16,4096]{2,1,0:T(8,128)(2,1)S(1)}, u32[]{:S(2)}, u32[]{:S(2)}) collective-permute-start(bf16[2,16,4096]{2,1,0:T(8,128)(2,1)} %param.5), channel_id=1, source_target_pairs={{0,7},{1,0},{2,1},{3,2},{4,3},{5,4},{6,5},{7,6},{8,15},{9,8},{10,9... | collective-permute-start | bytes 786440 | tf_op jit(solution)/shard_map/ppermute | solution.py:20
  8.4 0.8 slice_bitcast_fusion.1
  9.2 3.3 %collective-permute-done.1 = bf16[2,16,4096]{2,1,0:T(8,128)(2,1)S(1)} collective-permute-done((bf16[2,16,4096]{2,1,0:T(8,128)(2,1)S(1)}, bf16[2,16,4096]{2,1,0:T(8,128)(2,1)S(1)}, u32[]{:S(2)}, u32[]{:S(2)}) %collective-permute-start.1) | collective-permute-done | bytes 262176 | tf_op jit(solution)/shard_map/ppermute | solution.py:18
  12.5 0.9 convolution_bitcast_fusion
  13.4 1.8 %collective-permute-start.5 = (bf16[2,16,4096]{2,1,0:T(8,128)(2,1)S(1)}, bf16[2,16,4096]{2,1,0:T(8,128)(2,1)S(1)}, u32[]{:S(2)}, u32[]{:S(2)}) collective-permute-start(bf16[2,16,4096]{2,1,0:T(8,128)(2,1)S(1)} %collective-permute-done.4), channel_id=1, source_target_pairs={{0,7},{1,0},{2,1},{3,2},{4,3},{5,4},{6,5},{7,6},{8,15},{9,8},{10,9... | collective-permute-start | bytes 786440 | tf_op jit(solution)/shard_map/ppermute | solution.py:20
  15.2 3.1 %collective-permute-done.2 = bf16[2,16,4096]{2,1,0:T(8,128)(2,1)S(1)} collective-permute-done((bf16[2,16,4096]{2,1,0:T(8,128)(2,1)S(1)}, bf16[2,16,4096]{2,1,0:T(8,128)(2,1)S(1)}, u32[]{:S(2)}, u32[]{:S(2)}) %collective-permute-start.2) | collective-permute-done | bytes 262176 | tf_op jit(solution)/shard_map/ppermute | solution.py:18
  18.4 0.7 collective-permute-done.5
  19.1 1.9 %collective-permute-start.6 = (bf16[2,16,4096]{2,1,0:T(8,128)(2,1)S(1)}, bf16[2,16,4096]{2,1,0:T(8,128)(2,1)S(1)}, u32[]{:S(2)}, u32[]{:S(2)}) collective-permute-start(bf16[2,16,4096]{2,1,0:T(8,128)(2,1)S(1)} %collective-permute-done.5), channel_id=1, source_target_pairs={{0,7},{1,0},{2,1},{3,2},{4,3},{5,4},{6,5},{7,6},{8,15},{9,8},{10,9... | collective-permute-start | bytes 786440 | tf_op jit(solution)/shard_map/ppermute | solution.py:20
  21.0 3.1 %collective-permute-done.3 = bf16[2,16,4096]{2,1,0:T(8,128)(2,1)S(1)} collective-permute-done((bf16[2,16,4096]{2,1,0:T(8,128)(2,1)S(1)}, bf16[2,16,4096]{2,1,0:T(8,128)(2,1)S(1)}, u32[]{:S(2)}, u32[]{:S(2)}) %collective-permute-start.3) | collective-permute-done | bytes 262176 | tf_op jit(solution)/shard_map/ppermute | solution.py:18
  24.2 1.0 constant_dynamic-update-slice_fusion.11
  25.5 0.5 fusion.3
  26.0 0.5 fusion.2
  26.4 0.4 add_convert_fusion
  26.9 0.5 slice-done
  27.4 1.5 slice-done.1
  28.9 1.3 fusion.1
  30.2 0.3 copy.12
  30.5 41.4 %all_to_all.33 = bf16[2,64,1024]{2,0,1:T(2,128)(2,1)S(1)} all-to-all(bf16[2,64,1024]{2,0,1:T(2,128)(2,1)S(1)} %copy.12), channel_id=1, replica_groups=mesh['day'=64,'pair'=8] {'day'}, dimensions={1} | all-to-all | bytes 524288 | tf_op jit(solution)/shard_map/all_to_all | solution.py:64
  71.9 0.2 convert_reduce_fusion
  72.2 0.6 broadcast_multiply_fusion
  73.6 0.2 fusion.20
  73.8 0.2 fusion.11
  74.1 0.5 broadcast.37
  74.6 0.8 reduce.6
  75.4 0.8 reshape.58
  76.2 5.8 %all-to-all-start.1 = ((bf16[64,2,1024]{2,1,0:T(2,128)(2,1)}), bf16[64,2,1024]{2,1,0:T(2,128)(2,1)S(1)}, u32[]{:S(2)}, u32[]{:S(2)}) async-start(bf16[64,2,1024]{2,1,0:T(2,128)(2,1)} %reshape.58), calls=%async_computation.1 | async-start | bytes 524288 | tf_op jit(solution)/shard_map/all_to_all | solution.py:76
  82.0 87.7 %all-gather = f32[64,1,1024]{2,1,0:T(1,128)S(1)} all-gather(f32[1,1,1024]{2,1,0:T(1,128)S(1)} %fusion.15), channel_id=1, replica_groups=mesh['day'=64,'pair'=8] {'day'}, dimensions={0}, use_global_device_ids=true | all-gather | bytes 266240 | tf_op jit(solution)/shard_map/all_gather | solution.py:79
  169.7 0.8 copy.19
  170.4 0.2 reshape.59
  170.6 1.5 reduce.4
  172.3 0.8 copy.15
  (37 shorter events, 0.9 us)
Async XLA Ops:
  0.6 24.7 %copy-start = (bf16[2,16,4096]{2,1,0:T(8,128)(2,1)S(1)}, bf16[2,16,4096]{2,1,0:T(8,128)(2,1)}, u32[]{:S(2)}) copy-start(bf16[2,16,4096]{2,1,0:T(8,128)(2,1)} %param.5) | copy-start | bytes 786436
  0.6 6.0 %collective-permute-start = (bf16[2,16,4096]{2,1,0:T(8,128)(2,1)}, bf16[2,16,4096]{2,1,0:T(8,128)(2,1)S(1)}, u32[]{:S(2)}, u32[]{:S(2)}) collective-permute-start(bf16[2,16,4096]{2,1,0:T(8,128)(2,1)} %param.5), channel_id=1, source_target_pairs={{0,1},{1,2},{2,3},{3,4},{4,5},{5,6},{6,7},{7,0},{8,9},{9,10},{10,1... | collective-permute-start | bytes 786440 | tf_op jit(solution)/shard_map/ppermute | solution.py:18
  6.7 5.8 %collective-permute-start.1 = (bf16[2,16,4096]{2,1,0:T(8,128)(2,1)S(1)}, bf16[2,16,4096]{2,1,0:T(8,128)(2,1)S(1)}, u32[]{:S(2)}, u32[]{:S(2)}) collective-permute-start(bf16[2,16,4096]{2,1,0:T(8,128)(2,1)S(1)} %collective-permute-done), channel_id=1, source_target_pairs={{0,1},{1,2},{2,3},{3,4},{4,5},{5,6},{6,7},{7,0},{8,9},{9,10},{10,1... | collective-permute-start | bytes 786440 | tf_op jit(solution)/shard_map/ppermute | solution.py:18
  6.7 6.8 %collective-permute-start.4 = (bf16[2,16,4096]{2,1,0:T(8,128)(2,1)}, bf16[2,16,4096]{2,1,0:T(8,128)(2,1)S(1)}, u32[]{:S(2)}, u32[]{:S(2)}) collective-permute-start(bf16[2,16,4096]{2,1,0:T(8,128)(2,1)} %param.5), channel_id=1, source_target_pairs={{0,7},{1,0},{2,1},{3,2},{4,3},{5,4},{6,5},{7,6},{8,15},{9,8},{10,9... | collective-permute-start | bytes 786440 | tf_op jit(solution)/shard_map/ppermute | solution.py:20
  12.5 5.8 %collective-permute-start.2 = (bf16[2,16,4096]{2,1,0:T(8,128)(2,1)S(1)}, bf16[2,16,4096]{2,1,0:T(8,128)(2,1)S(1)}, u32[]{:S(2)}, u32[]{:S(2)}) collective-permute-start(bf16[2,16,4096]{2,1,0:T(8,128)(2,1)S(1)} %collective-permute-done.1), channel_id=1, source_target_pairs={{0,1},{1,2},{2,3},{3,4},{4,5},{5,6},{6,7},{7,0},{8,9},{9,10},{10,1... | collective-permute-start | bytes 786440 | tf_op jit(solution)/shard_map/ppermute | solution.py:18
  13.4 5.7 %collective-permute-start.5 = (bf16[2,16,4096]{2,1,0:T(8,128)(2,1)S(1)}, bf16[2,16,4096]{2,1,0:T(8,128)(2,1)S(1)}, u32[]{:S(2)}, u32[]{:S(2)}) collective-permute-start(bf16[2,16,4096]{2,1,0:T(8,128)(2,1)S(1)} %collective-permute-done.4), channel_id=1, source_target_pairs={{0,7},{1,0},{2,1},{3,2},{4,3},{5,4},{6,5},{7,6},{8,15},{9,8},{10,9... | collective-permute-start | bytes 786440 | tf_op jit(solution)/shard_map/ppermute | solution.py:20
  18.3 5.8 %collective-permute-start.3 = (bf16[2,16,4096]{2,1,0:T(8,128)(2,1)S(1)}, bf16[2,16,4096]{2,1,0:T(8,128)(2,1)S(1)}, u32[]{:S(2)}, u32[]{:S(2)}) collective-permute-start(bf16[2,16,4096]{2,1,0:T(8,128)(2,1)S(1)} %collective-permute-done.2), channel_id=1, source_target_pairs={{0,1},{1,2},{2,3},{3,4},{4,5},{5,6},{6,7},{7,0},{8,9},{9,10},{10,1... | collective-permute-start | bytes 786440 | tf_op jit(solution)/shard_map/ppermute | solution.py:18
  19.1 6.1 %collective-permute-start.6 = (bf16[2,16,4096]{2,1,0:T(8,128)(2,1)S(1)}, bf16[2,16,4096]{2,1,0:T(8,128)(2,1)S(1)}, u32[]{:S(2)}, u32[]{:S(2)}) collective-permute-start(bf16[2,16,4096]{2,1,0:T(8,128)(2,1)S(1)} %collective-permute-done.5), channel_id=1, source_target_pairs={{0,7},{1,0},{2,1},{3,2},{4,3},{5,4},{6,5},{7,6},{8,15},{9,8},{10,9... | collective-permute-start | bytes 786440 | tf_op jit(solution)/shard_map/ppermute | solution.py:20
  25.3 2.2 %slice-start = ((s8[8388608]{0:T(1024)(128)(4,1)}), s8[4194304]{0:T(1024)(128)(4,1)S(1)}, s32[]{:S(2)}) async-start(s8[8388608]{0:T(1024)(128)(4,1)} %bitcast.35), calls=%async_computation.2 | async-start | bytes 8388608
  25.9 2.9 %slice-start.1 = ((s8[8388608]{0:T(1024)(128)(4,1)}), s8[4194304]{0:T(1024)(128)(4,1)S(1)}, s32[]{:S(2)}) async-start(s8[8388608]{0:T(1024)(128)(4,1)} %bitcast.35), calls=%async_computation.3 | async-start | bytes 8388608
  28.9 44.6 %copy-start.1 = (bf16[128,128]{1,0:T(8,128)(2,1)S(1)}, bf16[128,128]{1,0:T(8,128)(2,1)}, u32[]{:S(2)}) copy-start(bf16[128,128]{1,0:T(8,128)(2,1)} %constant.56) | copy-start | bytes 98308
  76.2 94.2 %all-to-all-start.1 = ((bf16[64,2,1024]{2,1,0:T(2,128)(2,1)}), bf16[64,2,1024]{2,1,0:T(2,128)(2,1)S(1)}, u32[]{:S(2)}, u32[]{:S(2)}) async-start(bf16[64,2,1024]{2,1,0:T(2,128)(2,1)} %reshape.58), calls=%async_computation.1 | async-start | bytes 524288 | tf_op jit(solution)/shard_map/all_to_all | solution.py:76
